TPU v7x, 512 devices: a whole 4x8x8 slice. The times are simulated.
512 devices in a mesh: row: 64 (over y, x, core), col: 8 (over z).
Axes of the slice: x: 4, y: 8, z: 8, core: 2. Of those that a mesh axis runs over, the one named last changes fastest.
Arguments:
- panel_u: bfloat16 [64, 2560, 128], P('row'), may hold values from -0.125 to 0.125
- panel_v: bfloat16 [64, 2560, 128], P('row', 'col'), may hold values from -0.25 to 0.25
- linv: bfloat16 [2560, 2560], P('row', 'col')
- trail_u: bfloat16 [64, 16, 2560, 128], P('row', 'col'), may hold values from -0.125 to 0.125
- trail_v: bfloat16 [64, 16, 2560, 128], P('row', 'col'), may hold values from -0.125 to 0.125
- rank_map: int32 [64, 64], replicated, may hold values from 32 to 128, as said below
- tile_of_slot: int32 [64], replicated, may hold values from 0 to 63, each once
- band_cols: int32 [16], P('col'), may hold values from 0 to 63, as said below
Outputs:
- gram_left: float32 [64, 16, 256, 256], P('row', 'col')
- gram_right: float32 [64, 16, 256, 256], P('row', 'col')
Inputs may be any that keep to these rules, and one draw needn't show every extreme that they name: rank_map[i, j] for j != i is the rank of trailing tile (i, j), including band tiles with j > i, whose core is zero; rank_map[i, i] is the rank of panel tile i; some panel tile has rank 128. `tile_of_slot`: a permutation. `band_cols`: distinct values.
All inputs are finite; a program needn't handle non-finite values.
Results may differ from a plain program's by a relative error of at most 0.0049.
Values may be sent and summed in bfloat16 or wider, within the bound.
A program may use at most 64 MiB of HBM per device.

v0:
```python
import jax
import jax.numpy as jnp
from jax import lax
from jax.sharding import PartitionSpec as P


def broadcast(block, axis, holder):
    block = jnp.where(lax.axis_index(axis) == holder, block, jnp.zeros_like(block))
    return lax.psum(block, axis)


def cross_rows(first, second):
    return lax.dot_general(
        first, second, (((0,), (0,)), ((), ())), preferred_element_type=jnp.float32
    )


def shards(panel_u, panel_v, linv, trail_u, trail_v, rank_map, tile_of_slot, band_cols):
    tile_count = tile_of_slot.shape[0]
    rank_width = panel_u.shape[2]
    band_width = band_cols.shape[0]
    slot_ids = jnp.arange(tile_count, dtype=jnp.int32)
    row_ids = slot_ids[:, None]
    col_ids = slot_ids[None, :]
    columns = jnp.arange(rank_width, dtype=jnp.int32)

    def rank_lookup(first_tile, second_tile):
        return jnp.sum(jnp.where((row_ids == first_tile) & (col_ids == second_tile), rank_map, 0))

    own_slot = lax.axis_index("row")
    own_tile = jnp.sum(jnp.where(slot_ids == own_slot, tile_of_slot, 0))
    own_keep = (columns < rank_lookup(own_tile, own_tile))[None, :]
    own_basis = jnp.where(own_keep, panel_u[0], jnp.zeros_like(panel_u[0]))
    own_right = jnp.where(own_keep, panel_v[0], jnp.zeros_like(panel_v[0]))
    band_tiles = [band_cols[band_slot] for band_slot in range(band_width)]
    sources = [
        jnp.sum(jnp.where(tile_of_slot == band_tile, slot_ids, 0)) for band_tile in band_tiles
    ]
    partial_value = jnp.dot(
        lax.all_gather(linv, "row", axis=0, tiled=True),
        own_right,
        preferred_element_type=jnp.float32,
    )
    solved = lax.psum(partial_value, "col").astype(jnp.bfloat16)
    pairs = [
        (
            broadcast(own_basis, "row", sources[band_slot]),
            broadcast(solved, "row", sources[band_slot]),
        )
        for band_slot in range(band_width)
    ]
    bases = [pair_now[0] for pair_now in pairs]
    weights = [pair_now[1] for pair_now in pairs]
    left_grams = []
    right_grams = []
    for band_slot in range(band_width):
        band_tile = band_tiles[band_slot]
        core_mat = cross_rows(solved, weights[band_slot])
        core_mat = jnp.where(band_tile < own_tile, core_mat, jnp.zeros_like(core_mat)).astype(
            jnp.bfloat16
        )
        update = jnp.dot(bases[band_slot], core_mat.T, preferred_element_type=jnp.float32).astype(
            jnp.bfloat16
        )
        trail_keep = (columns < rank_lookup(own_tile, band_tile))[None, :]
        kept_u = jnp.where(trail_keep, trail_u[0, band_slot], jnp.zeros_like(update))
        kept_v = jnp.where(trail_keep, trail_v[0, band_slot], jnp.zeros_like(update))
        left_stack = jnp.concatenate([kept_u, own_basis], axis=1)
        right_stack = jnp.concatenate([kept_v, -update], axis=1)
        left_grams.append(cross_rows(left_stack, left_stack))
        right_grams.append(cross_rows(right_stack, right_stack))
    return (jnp.stack(left_grams, axis=0)[None], jnp.stack(right_grams, axis=0)[None])


def solution(mesh):
    return jax.shard_map(
        shards,
        mesh=mesh,
        in_specs=(
            P("row", None, None),
            P("row", "col", None),
            P("row", "col"),
            P("row", "col", None, None),
            P("row", "col", None, None),
            P(),
            P(),
            P("col"),
        ),
        out_specs=(P("row", "col", None, None), P("row", "col", None, None)),
        check_vma=False,
    )
```

profile of v0, /device:TPU:25, one launch (start us, length us, event | category | flops | bytes accessed | tf_op | source)
XLA Modules:
  0.0 376.5 jit_solution(1439568400219508814)
XLA Ops:
  8.0 1.3 fusion.42
  9.3 2.7 fusion.31
  13.2 1.3 copy.11
  14.6 1.1 copy.15
  15.7 1.4 fusion.40
  17.1 1.1 copy.17
  20.1 0.8 select_reduce_fusion.2
  21.6 1.3 iota_compare_fusion.1
  22.8 1.0 broadcast_select_fusion.3
  23.8 0.9 copy-done
  24.7 0.9 broadcast_select_fusion.1
  25.6 71.9 %all-gather.2.cloned.1.call-done = bf16[2560,320]{1,0:T(8,128)(2,1)} async-done(((bf16[40,320]{1,0:T(8,128)(2,1)}), bf16[2560,320]{1,0:T(8,128)(2,1)}) %all-gather.2.cloned.1.call-update) | async-done | bytes 1638416 | tf_op jit(solution)/shard_map/all_gather | solution.py:40
  97.5 2.3 convolution_bitcast_fusion
  99.8 51.0 %all-reduce.5 = bf16[2560,128]{0,1:T(8,128)(2,1)S(1)} all-reduce(f32[2560,128]{0,1:T(8,128)S(1)} %convolution_bitcast_fusion), channel_id=1, replica_groups=mesh['row'=64,'col'=8] {'col'}, use_global_device_ids=true, to_apply=%region_6.7 | all-reduce | flops 327680 | bytes 1966080 | tf_op jit(solution)/shard_map/psum | solution.py:44
  150.8 1.2 broadcast_select_fusion.2
  152.1 1.1 copy-done.2
  153.3 1.2 bitcast_select_fusion.1
  158.2 1.8 fusion.21
  160.0 1.0 bitcast_select_fusion
  161.5 0.8 maximum_bitcast_fusion
  162.3 201.3 %all-reduce.4.cloned.1.call-done = (bf16[2560,128]{0,1:T(8,128)(2,1)}, bf16[2560,128]{0,1:T(8,128)(2,1)}, bf16[2560,128]{0,1:T(8,128)(2,1)}, bf16[2560,128]{0,1:T(8,128)(2,1)}) async-done(((bf16[2560,128]{0,1:T(8,128)(2,1)}, bf16[2560,128]{0,1:T(8,128)(2,1)}, bf16[2560,128]{0,1:T(8,128)(2,1)}, bf16[2560,128]{0,1:T(8,128)(2,1)}), (bf16[2560,128]{0,1:T(8,128)(2,1)}, bf16[2560,128]{0,1:T(8,128)(2,1)}, ...) | async-done | bytes 2621456 | tf_op jit(solution)/shard_map/psum | solution.py:9
  363.6 2.3 fusion
  367.2 0.9 fusion.1
  368.8 0.8 maximum_bitcast_fusion.1
  (34 shorter events, 7.2 us)
Async XLA Ops:
  7.2 7.4 %copy-start.4 = (bf16[1,2,2560,128]{3,2,1,0:T(8,128)(2,1)S(1)}, bf16[1,2,2560,128]{3,2,1,0:T(8,128)(2,1)}, u32[]{:S(2)}) copy-start(bf16[1,2,2560,128]{3,2,1,0:T(8,128)(2,1)} %param.11) | copy-start | bytes 3932164
  7.2 90.3 %all-gather.2.cloned.1.call-start = ((), (), s32[]{:S(2)}) async-start(), calls=%async_computation | async-start | bytes 1996800 | tf_op jit(solution)/shard_map/all_gather | solution.py:40
  7.9 355.7 %all-reduce.4.cloned.1.call-start = ((), (), s32[]{:S(2)}) async-start(), calls=%async_computation.1 | async-start | bytes 5242880 | tf_op jit(solution)/shard_map/psum | solution.py:9
  17.1 3.1 copy-start.10
  22.8 74.6 %copy-start.9 = (bf16[1,320,128]{2,1,0:T(8,128)(2,1)S(1)}, bf16[1,320,128]{2,1,0:T(8,128)(2,1)}, u32[]{:S(2)}) copy-start(bf16[1,320,128]{2,1,0:T(8,128)(2,1)} %param.9) | copy-start | bytes 245764
  23.8 0.9 copy-start
  152.0 1.1 copy-start.2
  152.0 1.3 copy-start.3
  157.1 1.1 copy-start.1
  363.6 2.3 copy-start.7
  365.9 1.1 copy-start.5
  365.9 1.3 copy-start.6
  367.2 1.1 copy-start.8
Sparse Core Ops, SparseCore 0:
  11.3 86.1 all-gather.1
  152.2 211.4 all-reduce.3
where the time goes:
time: 377 us; the launch traced here: 376 us
  waiting for transfers between devices  274 us (73%)
  blocking collectives  51 us (14%)
  between operations  18 us (5%)
  other arithmetic  14.2 us (4%)
  local copies, waits for them, and re-layouts  10.4 us (3%)
  matrix products  8.9 us (2%)
    psum x1, waiting for transfers between devices, broadcast(): return lax.psum(block, axis)  201 us
    all_gather x1, waiting for transfers between devices, shards(): lax.all_gather(linv, 'row', axis=0, tiled=True)  71.9 us
    psum x1, blocking collectives, shards(): solved = lax.psum(partial_value, 'col').astype(jnp.bfloat16)  51 us
    unnamed x27, local copies, waits for them, and re-layouts  7.61 us
  transfers between devices with their start and end apart: 2, of which 2 were waited for; matrix products, arithmetic and copies ran while one was open for 6% of the time, Pallas kernels for 0%

commit v1 on v0

v1 whole, which is shorter than its diff:
```python
import functools

import jax
import jax.numpy as jnp
from jax import lax
from jax.experimental import pallas as pl
from jax.experimental.pallas import tpu as pltpu
from jax.sharding import PartitionSpec as P

MESH = pl.DeviceIdType.MESH
BF = jnp.bfloat16
F32 = jnp.float32
HI = lax.Precision.HIGHEST


def near_first(n):
    return sorted(range(1, n), key=lambda d: (min(d, n - d), d))


def cross_rows(first, second):
    return lax.dot_general(first, second, (((0,), (0,)), ((), ())), preferred_element_type=F32)


def flag_row(shape_like, cond):
    return jnp.where(cond, jnp.ones(shape_like, F32), jnp.zeros(shape_like, F32))


def plan(ny, nx, nz):
    counts = dict(
        v=1, usib=1, bc=nz, ly=ny, lx=ny * nx, zs=nz, ub=nx, uc=ny, ud=ny, ue=nx, uf=1,
        yx=nx, yy=ny, yg=ny, yh=nx, pc=nz, zc=nz,
    )
    base, total = {}, 0
    for name, count in counts.items():
        base[name] = total
        total += count
    return base, total


def kernel(
    dims,
    panel_u, panel_v, linv, trail_u, trail_v, rank_map, tile_of_slot, band_cols, band_rows,
    gram_left, gram_right,
    basis, basis_sib, chosen, ux, ured, uy, upiece, uband, tu, tv,
    vchip, lbuf, zsend, zrecv, sol, selx, bsel, yrecv, yred, yg, bcbuf,
    pown, psend, psib, csend, crecv, right,
    ssem, rsem, lsem,
):
    ny, nx, nz = dims
    base, _ = plan(ny, nx, nz)
    points, rank = basis.shape
    depth = linv.shape[0]
    row = lax.axis_index("row")
    z = lax.axis_index("col")
    y, x, h = row // (2 * nx), (row // 2) % nx, row % 2
    sib = 1 - h
    spot = lambda yy, xx, hh: (yy * nx + xx) * 2 + hh

    def to_y(d):
        return {"row": spot((y + d) % ny, x, h), "col": z}

    def to_x(d):
        return {"row": spot(y, (x + d) % nx, h), "col": z}

    def to_z(d):
        return {"row": row, "col": (z + d) % nz}

    to_sib = {"row": spot(y, x, sib), "col": z}

    def copy(src, dst, name, k, where, rk=None):
        return pltpu.make_async_remote_copy(
            src_ref=src, dst_ref=dst,
            send_sem=ssem.at[base[name] + k],
            recv_sem=rsem.at[base[name] + (k if rk is None else rk)],
            device_id=where, device_id_type=MESH,
        )

    barrier = pltpu.get_barrier_semaphore()
    peers = [to_y(d) for d in near_first(ny)] + [to_x(d) for d in near_first(nx)]
    peers += [to_z(d) for d in near_first(nz)] + [to_sib]
    for peer in peers:
        pl.semaphore_signal(barrier, inc=1, device_id=peer, device_id_type=MESH)

    load_u = pltpu.make_async_copy(trail_u.at[0], tu, lsem.at[0])
    load_v = pltpu.make_async_copy(trail_v.at[0], tv, lsem.at[1])
    load_u.start()
    load_v.start()

    lanes = lax.broadcasted_iota(jnp.int32, (1, rank), 1)
    own_tile = tile_of_slot[row]
    own_mask = flag_row((1, rank), lanes < rank_map[own_tile, own_tile]).astype(BF)
    mine = pl.multiple_of(h * rank, rank)
    vchip[:, pl.ds(mine, rank)] = panel_v[0] * own_mask
    lbuf[y, x] = linv[...]
    bcbuf[z] = band_rows[...]
    step = points // 4
    for k in range(4):
        basis[k * step:(k + 1) * step, :] = panel_u[0, k * step:(k + 1) * step, :] * own_mask

    pl.semaphore_wait(barrier, len(peers))

    waits = []
    cv = copy(vchip.at[:, pl.ds(mine, rank)], vchip.at[:, pl.ds(mine, rank)], "v", 0, to_sib)
    cv.start()
    waits.append(cv)
    ly = {}
    for d in near_first(ny):
        ly[d] = copy(linv, lbuf.at[y, x], "ly", d, to_y(d))
        ly[d].start()
    bcs = {}
    for d in near_first(nz):
        bcs[d] = copy(band_rows, bcbuf.at[z], "bc", d, to_z(d))
        bcs[d].start()
    cu = copy(basis, basis_sib, "usib", 0, to_sib)
    cu.start()

    lx = {}

    def forward(d):
        yy = (y - d) % ny
        src = linv if d == 0 else lbuf.at[yy, x]
        for dx in near_first(nx):
            lx[d, dx] = copy(src, lbuf.at[yy, x], "lx", d * nx + dx, to_x(dx))
            lx[d, dx].start()

    order_y = [0] + near_first(ny)
    forward(0)
    for d in near_first(ny):
        ly[d].wait_recv()
        forward(d)

    cu.wait_recv()
    band_tile = band_cols[h]
    f_own = flag_row((1, rank), jnp.broadcast_to(own_tile == band_tile, (1, rank))).astype(BF)
    sib_tile = tile_of_slot[spot(y, x, sib)]
    f_sib = flag_row((1, rank), jnp.broadcast_to(sib_tile == band_tile, (1, rank))).astype(BF)
    px = points // nx
    for k in range(nx):
        part = slice(k * px, (k + 1) * px)
        chosen[k] = basis[part, :] * f_own + basis_sib[part, :] * f_sib
    ub = {}
    for d in near_first(nx):
        ub[d] = copy(chosen.at[(x + d) % nx], ux.at[x], "ub", d, to_x(d))
        ub[d].start()

    cv.wait_recv()
    zs = {}
    for d in order_y:
        yy = (y - d) % ny
        for dx in near_first(nx):
            lx[d, dx].wait_recv()
        block = lbuf[yy].astype(F32).reshape(nx * depth, linv.shape[1]).astype(BF)
        part = jnp.dot(block, vchip[...], preferred_element_type=F32)
        part = part.reshape(nx, depth, 2 * rank).astype(BF)
        zsend[d] = part
        e = (yy + nz - z) % nz
        zs[d] = copy(zsend.at[d], zrecv.at[z], "zs", d, {"row": row, "col": yy}, rk=e)

        @pl.when(e != 0)
        def _():
            zs[d].start()

        @pl.when(e == 0)
        def _():
            zrecv[z] = part

    for d in near_first(nx):
        ub[d].wait_recv()
    total = chosen[x]
    for d in range(1, nx):
        total = total + ux[(x + d) % nx]
    py = px // ny
    ured[...] = total.reshape(ny, py, rank)
    uc = {}
    for d in near_first(ny):
        uc[d] = copy(ured.at[(y + d) % ny], uy.at[y], "uc", d, to_y(d))
        uc[d].start()

    load_u.wait()
    chunk = points // 5
    keeps = [
        flag_row((1, rank), lanes < rank_map[own_tile, band_cols[i]]).astype(BF) for i in range(2)
    ]

    def left_gram(i):
        gram_left[0, i] = jnp.zeros((2 * rank, 2 * rank), F32)

        def body(k, carry):
            rows = pl.ds(pl.multiple_of(k * chunk, 16), chunk)
            both = jnp.concatenate([tu[i, rows, :] * keeps[i], basis[rows, :]], axis=1)
            gram_left[0, i] += cross_rows(both, both)
            return carry

        lax.fori_loop(0, 5, body, 0)

    left_gram(0)

    for d in near_first(ny):
        uc[d].wait_recv()
    total = ured[y]
    for d in range(1, ny):
        total = total + uy[(y + d) % ny]
    my_piece = pl.ds(pl.multiple_of((x * ny + y) * py, 16), py)
    my_slab = pl.ds(pl.multiple_of(x * px, 16), px)
    upiece[...] = total
    uband[h, my_piece, :] = total
    ud = {}
    for d in near_first(ny):
        ud[d] = copy(upiece, uband.at[h, my_piece, :], "ud", d, to_y(d))
        ud[d].start()

    for e in range(1, nz):
        copy(zsend.at[0], zrecv.at[z], "zs", 0, to_z(1), rk=e).wait_recv()
    acc = zrecv[0].astype(F32)
    for k in range(1, nz):
        acc = acc + zrecv[k].astype(F32)
    sol[...] = acc.astype(BF)
    yx = {}
    for d in near_first(nx):
        yx[d] = copy(sol.at[(x + d) % nx], selx.at[x], "yx", d, to_x(d))
        yx[d].start()
    selx[x] = sol[x]

    for d in near_first(ny):
        ud[d].wait_recv()
    ue = {}
    for d in near_first(nx):
        ue[d] = copy(uband.at[h, my_slab, :], uband.at[h, my_slab, :], "ue", d, to_x(d))
        ue[d].start()

    for d in near_first(nz):
        bcs[d].wait_recv()
    for d in near_first(nx):
        yx[d].wait_recv()
    tiles = [tile_of_slot[spot(y, k // 2, k % 2)] for k in range(2 * nx)]
    blocks = [
        selx[k // 2, :, (k % 2) * rank:(k % 2 + 1) * rank].astype(F32) for k in range(2 * nx)
    ]
    for p in range(nz):
        for i in range(2):
            name_row = bcbuf[p][i:i + 1, :]
            got = jnp.zeros((depth, rank), F32)
            for k in range(2 * nx):
                got = got + blocks[k] * flag_row((1, rank), name_row == tiles[k])
            bsel[p, :, i * rank:(i + 1) * rank] = got.astype(BF)
    yy_copies = {}
    for d in near_first(ny):
        yy_copies[d] = copy(bsel.at[(y + d) % ny], yrecv.at[y], "yy", d, to_y(d))
        yy_copies[d].start()
    yrecv[y] = bsel[y]
    for d in near_first(ny):
        yy_copies[d].wait_recv()
    acc = yrecv[0].astype(F32)
    for k in range(1, ny):
        acc = acc + yrecv[k].astype(F32)
    yred[...] = acc.astype(BF)
    yg[x, y] = acc.astype(BF)
    ygc = {}
    for d in near_first(ny):
        ygc[d] = copy(yred, yg.at[x, y], "yg", d, to_y(d))
        ygc[d].start()

    for d in near_first(nx):
        ue[d].wait_recv()
    uf = copy(uband.at[h], uband.at[h], "uf", 0, to_sib)
    uf.start()

    for d in near_first(ny):
        ygc[d].wait_recv()
    yh = {}
    for d in near_first(nx):
        yh[d] = copy(yg.at[x], yg.at[x], "yh", d, to_x(d))
        yh[d].start()

    left_gram(1)
    load_v.wait()
    uf.wait_recv()

    def right_gram(i):
        right[i] = jnp.zeros((2 * rank, 2 * rank), F32)

        def body(k, carry):
            rows = pl.ds(pl.multiple_of(k * chunk, 16), chunk)
            both = jnp.concatenate([tv[i, rows, :] * keeps[i], uband[i, rows, :]], axis=1)
            right[i] += cross_rows(both, both)
            return carry

        lax.fori_loop(0, 5, body, 0)

    right_gram(0)

    for d in near_first(nx):
        yh[d].wait_recv()
    sol_rows = sol[...].astype(F32).reshape(nx * depth, 2 * rank).astype(BF)
    order_z = near_first(nz) + [0]
    pcs = {}
    for e in order_z:
        p = (z + e) % nz
        y_rows = jnp.concatenate([yg[k, p].astype(F32) for k in range(nx)], axis=0).astype(BF)
        part = cross_rows(sol_rows, y_rows)
        low, high = part[:rank], part[rank:]
        pown[e] = jnp.where(h == 0, low, high)
        psend[e] = jnp.where(h == 0, high, low)
        pcs[e] = copy(psend.at[e], psib.at[e], "pc", e, to_sib)
        pcs[e].start()
    zc = {}
    for e in order_z:
        pcs[e].wait_recv()
        csum = (pown[e] + psib[e]).astype(BF)
        if e == 0:
            crecv[z] = csum
        else:
            csend[e] = csum
            zc[e] = copy(csend.at[e], crecv.at[z], "zc", e, to_z(e))
            zc[e].start()

    right_gram(1)

    for e in near_first(nz):
        zc[e].wait_recv()
    core = crecv[0].astype(F32)
    for k in range(1, nz):
        core = core + crecv[k].astype(F32)
    for i in range(2):
        lower = flag_row((1, rank), jnp.broadcast_to(band_cols[i] < own_tile, (1, rank)))
        c = (core[:, i * rank:(i + 1) * rank] * lower).astype(BF).astype(F32)
        g = right[i, :rank, rank:]
        gram_uu = right[i, rank:, rank:]
        cross = -lax.dot_general(g, c, (((1,), (1,)), ((), ())), precision=HI, preferred_element_type=F32)
        crossed = -lax.dot_general(c, g, (((1,), (1,)), ((), ())), precision=HI, preferred_element_type=F32)
        half = jnp.dot(c, gram_uu, precision=HI, preferred_element_type=F32)
        corner = lax.dot_general(half, c, (((1,), (1,)), ((), ())), precision=HI, preferred_element_type=F32)
        gram_right[0, i, :rank, :rank] = right[i, :rank, :rank]
        gram_right[0, i, :rank, rank:] = cross
        gram_right[0, i, rank:, :rank] = crossed
        gram_right[0, i, rank:, rank:] = corner

    for group in (ly, bcs, lx, ub, uc, ud, yx, ue, yy_copies, ygc, yh, pcs, zc):
        for one in group.values():
            one.wait_send()
    for one in (cv, cu, uf):
        one.wait_send()
    for d in order_y:
        yy = (y - d) % ny

        @pl.when((yy + nz - z) % nz != 0)
        def _():
            zs[d].wait_send()


def shards(dims, panel_u, panel_v, linv, trail_u, trail_v, rank_map, tile_of_slot, band_cols):
    ny, nx, nz = dims
    points, rank = panel_u.shape[1:]
    depth, width = linv.shape
    px = points // nx
    py = px // ny
    _, total = plan(ny, nx, nz)
    band_rows = jnp.broadcast_to(jnp.tile(band_cols, 4)[:, None], (8, rank))
    vmem = pl.BlockSpec(memory_space=pltpu.VMEM)
    smem = pl.BlockSpec(memory_space=pltpu.SMEM)
    hbm = pl.BlockSpec(memory_space=pl.ANY)
    out = jax.ShapeDtypeStruct((1, 2, 2 * rank, 2 * rank), F32)
    scratch = [
        pltpu.VMEM((points, rank), BF),
        pltpu.VMEM((points, rank), BF),
        pltpu.VMEM((nx, px, rank), BF),
        pltpu.VMEM((nx, px, rank), BF),
        pltpu.VMEM((ny, py, rank), BF),
        pltpu.VMEM((ny, py, rank), BF),
        pltpu.VMEM((py, rank), BF),
        pltpu.VMEM((2, points, rank), BF),
        pltpu.VMEM((2, points, rank), BF),
        pltpu.VMEM((2, points, rank), BF),
        pltpu.VMEM((width, 2 * rank), BF),
        pltpu.VMEM((ny, nx, depth, width), BF),
        pltpu.VMEM((ny, nx, depth, 2 * rank), BF),
        pltpu.VMEM((nz, nx, depth, 2 * rank), BF),
        pltpu.VMEM((nx, depth, 2 * rank), BF),
        pltpu.VMEM((nx, depth, 2 * rank), BF),
        pltpu.VMEM((nz, depth, 2 * rank), BF),
        pltpu.VMEM((ny, depth, 2 * rank), BF),
        pltpu.VMEM((depth, 2 * rank), BF),
        pltpu.VMEM((nx, nz, depth, 2 * rank), BF),
        pltpu.VMEM((nz, 8, rank), jnp.int32),
        pltpu.VMEM((nz, rank, 2 * rank), F32),
        pltpu.VMEM((nz, rank, 2 * rank), F32),
        pltpu.VMEM((nz, rank, 2 * rank), F32),
        pltpu.VMEM((nz, rank, 2 * rank), BF),
        pltpu.VMEM((nz, rank, 2 * rank), BF),
        pltpu.VMEM((2, 2 * rank, 2 * rank), F32),
        pltpu.SemaphoreType.DMA((total,)),
        pltpu.SemaphoreType.DMA((total,)),
        pltpu.SemaphoreType.DMA((2,)),
    ]
    return pl.pallas_call(
        functools.partial(kernel, dims),
        out_shape=(out, out),
        in_specs=[vmem, vmem, vmem, hbm, hbm, smem, smem, smem, vmem],
        out_specs=(vmem, vmem),
        scratch_shapes=scratch,
        compiler_params=pltpu.CompilerParams(
            collective_id=0, has_side_effects=True, vmem_limit_bytes=48 * 2**20
        ),
    )(panel_u, panel_v, linv, trail_u, trail_v, rank_map, tile_of_slot, band_cols, band_rows)


def solution(mesh):
    nz = mesh.shape["col"]
    ny = nz
    nx = mesh.shape["row"] // (2 * ny)
    return jax.shard_map(
        functools.partial(shards, (ny, nx, nz)),
        mesh=mesh,
        in_specs=(
            P("row", None, None),
            P("row", "col", None),
            P("row", "col"),
            P("row", "col", None, None),
            P("row", "col", None, None),
            P(),
            P(),
            P("col"),
        ),
        out_specs=(P("row", "col", None, None), P("row", "col", None, None)),
        check_vma=False,
    )
```

time: 377 us -> 99.2 us (0.26)
  the two profiles are of different devices: /device:TPU:25 before, /device:TPU:40 now
where the time goes in v1:
time: 99.2 us; the launch traced here: 98.8 us
  Pallas kernels  88.3 us (89%)
  local copies, waits for them, and re-layouts  9.83 us (10%)
    pallas_call x1, Pallas kernels, shards(): pl.pallas_call(functools.partial(kernel, dims), out_shape=(out, out), in_...  88.3 us
    unnamed x18, local copies, waits for them, and re-layouts  9.01 us

profile of v1, /device:TPU:40, one launch (start us, length us, event | category | flops | bytes accessed | tf_op | source)
XLA Modules:
  0.0 98.8 jit_solution(6372923260617901791)
XLA Ops:
  0.6 0.7 tile.2
  1.3 0.1 broadcast_in_dim.7
  1.4 0.1 broadcast_in_dim.8.band_rows
  1.4 0.0 copy-start
  1.4 1.3 %copy-done = bf16[1,2,2560,128]{3,2,1,0:T(8,128)(2,1)S(1)} copy-done((bf16[1,2,2560,128]{3,2,1,0:T(8,128)(2,1)S(1)}, bf16[1,2,2560,128]{3,2,1,0:T(8,128)(2,1)}, u32[]{:S(2)}) %copy-start) | copy-done | bytes 1310744
  2.8 0.0 copy-start.1
  2.8 1.3 %copy-done.1 = bf16[1,2,2560,128]{3,2,1,0:T(8,128)(2,1)S(1)} copy-done((bf16[1,2,2560,128]{3,2,1,0:T(8,128)(2,1)S(1)}, bf16[1,2,2560,128]{3,2,1,0:T(8,128)(2,1)}, u32[]{:S(2)}) %copy-start.1) | copy-done | bytes 1310744
  4.1 0.0 copy-start.2
  4.1 1.1 %copy-done.2 = bf16[1,2560,128]{2,1,0:T(8,128)(2,1)S(1)} copy-done((bf16[1,2560,128]{2,1,0:T(8,128)(2,1)S(1)}, bf16[1,2560,128]{2,1,0:T(8,128)(2,1)}, u32[]{:S(2)}) %copy-start.2) | copy-done | bytes 655384
  5.2 0.0 copy-start.3
  5.2 0.9 copy-done.3
  6.1 0.0 copy-start.4
  6.1 0.8 copy-done.4
  6.8 0.0 copy-start.5
  6.8 0.8 copy-done.5
  7.6 0.0 copy-start.6
  7.6 0.7 copy-done.6
  8.2 0.0 copy-start.7
  8.2 0.7 copy-done.7
  8.9 88.3 %shard_map.95 = (f32[1,2,256,256]{3,2,1,0:T(8,128)S(1)}, f32[1,2,256,256]{3,2,1,0:T(8,128)S(1)}) custom-call(bf16[1,2560,128]{2,1,0:T(8,128)(2,1)S(1)} %copy-done.2, bf16[1,320,128]{2,1,0:T(8,128)(2,1)S(1)} %copy-done.3, bf16[40,320]{1,0:T(8,128)(2,1)S(1)} %copy-done.5, bf16[1,2,2560,128]{3,2,1,0:T(8,128)(2,1)S(1)} %copy-done, ...), custom_call_target="tpu_custom_call" | custom-call | tf_op jit(solution)/shard_map/pallas_call | solution.py:395
  97.2 0.8 copy.12
  98.0 0.8 copy.13
Async XLA Ops:
  1.4 1.3 %copy-start = (bf16[1,2,2560,128]{3,2,1,0:T(8,128)(2,1)S(1)}, bf16[1,2,2560,128]{3,2,1,0:T(8,128)(2,1)}, u32[]{:S(2)}) copy-start(bf16[1,2,2560,128]{3,2,1,0:T(8,128)(2,1)} %trail_u.1) | copy-start | bytes 3932164
  2.8 1.3 %copy-start.1 = (bf16[1,2,2560,128]{3,2,1,0:T(8,128)(2,1)S(1)}, bf16[1,2,2560,128]{3,2,1,0:T(8,128)(2,1)}, u32[]{:S(2)}) copy-start(bf16[1,2,2560,128]{3,2,1,0:T(8,128)(2,1)} %trail_v.1) | copy-start | bytes 3932164
  4.1 1.1 %copy-start.2 = (bf16[1,2560,128]{2,1,0:T(8,128)(2,1)S(1)}, bf16[1,2560,128]{2,1,0:T(8,128)(2,1)}, u32[]{:S(2)}) copy-start(bf16[1,2560,128]{2,1,0:T(8,128)(2,1)} %panel_u.1) | copy-start | bytes 1966084
  5.2 0.9 copy-start.3
  6.1 0.8 copy-start.4
  6.8 0.8 copy-start.5
  7.6 0.7 copy-start.6
  8.2 0.7 copy-start.7

commit v2 on v0

v2 whole, which is shorter than its diff:
```python
import functools

import jax
import jax.numpy as jnp
from jax import lax
from jax.experimental import pallas as pl
from jax.experimental.pallas import tpu as pltpu
from jax.sharding import PartitionSpec as P

MESH = pl.DeviceIdType.MESH
BF = jnp.bfloat16
F32 = jnp.float32
HI = lax.Precision.HIGHEST


def near_first(n):
    return sorted(range(1, n), key=lambda d: (min(d, n - d), d))


def cross_rows(first, second):
    return lax.dot_general(first, second, (((0,), (0,)), ((), ())), preferred_element_type=F32)


def flag_row(shape_like, cond):
    return jnp.where(cond, jnp.ones(shape_like, F32), jnp.zeros(shape_like, F32))


def plan(ny, nx, nz):
    counts = dict(
        va=2 * nx, ua=2 * nx, vb=ny, ub=ny, vc=2 * nx, bc=nz, v=1, ly=ny, lx=ny * nx, zs=nz, zy=nz,
        gy=ny, gx=ny * nx, ut=1, ud=ny, ue=nx, uf=1, pc=ny, zc=nz,
    )
    base, total = {}, 0
    for name, count in counts.items():
        base[name] = total
        total += count
    return base, total


def kernel(
    dims,
    panel_u, panel_v, linv, trail_u, trail_v, rank_map, tile_of_slot, band_cols,
    gram_left, gram_right,
    basis, vown, vchip, vx, vsel, vy, vpiece, vband, ux, usel, uy, upiece, uband, tu, tv,
    lbuf, zsend, zrecv, sol, zysend, zyrecv, yg, bcbuf,
    pown, psend, psib, csend, crecv, right,
    ssem, rsem, lsem,
):
    ny, nx, nz = dims
    base, _ = plan(ny, nx, nz)
    points, rank = panel_u.shape[1:]
    depth, width = linv.shape
    py = width // nx
    row = lax.axis_index("row")
    z = lax.axis_index("col")
    y, x, h = row // (2 * nx), (row // 2) % nx, row % 2

    def spot(yy, xx, hh):
        return (yy * nx + xx) * 2 + hh

    def to_y(d):
        return {"row": spot((y + d) % ny, x, h), "col": z}

    def to_x(d, flip=0):
        return {"row": spot(y, (x + d) % nx, (h + flip) % 2), "col": z}

    def to_z(d):
        return {"row": row, "col": (z + d) % nz}

    to_sib = to_x(0, 1)
    to_turned = {"row": spot(z, x, h), "col": y}
    chips = [(0, 1)] + [(d, flip) for d in near_first(nx) for flip in (0, 1)]
    started = []

    def copy(src, dst, name, k, where, rk=None):
        return pltpu.make_async_remote_copy(
            src_ref=src, dst_ref=dst,
            send_sem=ssem.at[base[name] + k],
            recv_sem=rsem.at[base[name] + (k if rk is None else rk)],
            device_id=where, device_id_type=MESH,
        )

    def go(src, dst, name, k, where):
        one = copy(src, dst, name, k, where)
        one.start()
        started.append(one)
        return one

    def load(src, dst, k):
        one = pltpu.make_async_copy(src, dst, lsem.at[k])
        one.start()
        return one

    load_pv = load(panel_v.at[0], vown, 0)
    load_l = load(linv, lbuf.at[y, x], 1)
    load_pu = load(panel_u.at[0], basis, 2)

    barrier = pltpu.get_barrier_semaphore()
    peers = [to_y(d) for d in near_first(ny)] + [to_x(d, flip) for d, flip in chips]
    peers += [to_z(d) for d in near_first(nz)]
    for peer in peers:
        pl.semaphore_signal(barrier, inc=1, device_id=peer, device_id_type=MESH)

    @pl.when(y != z)
    def _():
        pl.semaphore_signal(barrier, inc=1, device_id=to_turned, device_id_type=MESH)

    load_tu = load(trail_u.at[0], tu, 3)
    load_tv = load(trail_v.at[0], tv, 4)

    lanes = lax.broadcasted_iota(jnp.int32, (1, rank), 1)
    own_tile = tile_of_slot[row]
    own_mask = flag_row((1, rank), lanes < rank_map[own_tile, own_tile]).astype(BF)
    mine = pl.multiple_of(h * rank, rank)
    odd = lax.broadcasted_iota(jnp.int32, (8, rank), 0) % 2
    bcbuf[z] = jnp.where(odd == 1, band_cols[1], band_cols[0])
    load_pv.wait()
    masked_v = vown[...] * own_mask
    vown[...] = masked_v
    vchip[:, pl.ds(mine, rank)] = masked_v
    load_pu.wait()
    step = points // 4
    for k in range(4):
        part = slice(k * step, (k + 1) * step)
        basis[part, :] = basis[part, :] * own_mask
    load_l.wait()

    pl.semaphore_wait(barrier, len(peers) + jnp.where(y != z, 1, 0))

    def quarter(k):
        return pl.ds(pl.multiple_of(k * py, 16), py)

    def uquarter(k):
        return pl.ds(pl.multiple_of(z * width + k * py, 16), py)

    va, ua, ly, bcs = {}, {}, {}, {}
    for d, flip in chips:
        xx = (x + d) % nx
        va[d, flip] = go(vown.at[quarter(xx), :], vx.at[x, h], "va", 2 * d + flip, to_x(d, flip))
    for d in near_first(nz):
        bcs[d] = go(bcbuf.at[z], bcbuf.at[z], "bc", d, to_z(d))
    for d in near_first(ny):
        ly[d] = go(lbuf.at[y, x], lbuf.at[y, x], "ly", d, to_y(d))
    cv = go(vchip.at[:, pl.ds(mine, rank)], vchip.at[:, pl.ds(mine, rank)], "v", 0, to_sib)
    for d, flip in chips:
        xx = (x + d) % nx
        ua[d, flip] = go(basis.at[uquarter(xx), :], ux.at[x, h], "ua", 2 * d + flip, to_x(d, flip))
    vx[x, h] = vown[quarter(x), :]
    ux[x, h] = basis[uquarter(x), :]

    lx = {}

    def forward_l(d):
        yy = (y - d) % ny
        for dx in near_first(nx):
            lx[d, dx] = go(lbuf.at[yy, x], lbuf.at[yy, x], "lx", d * nx + dx, to_x(dx))

    order_y = [0] + near_first(ny)
    forward_l(0)

    def pick(from_ref, to_ref):
        blocks = [from_ref[k // 2, k % 2] for k in range(2 * nx)]
        for p in range(nz):
            name_row = bcbuf[p, pl.ds(h, 1), :]
            got = jnp.zeros((py, rank), BF)
            for k in range(2 * nx):
                got = got + blocks[k] * flag_row((1, rank), name_row == tiles[k]).astype(BF)
            to_ref[p] = got

    def summed(ref, count):
        total = ref[0]
        for k in range(1, count):
            total = total + ref[k]
        return total

    tiles = [tile_of_slot[spot(y, k // 2, k % 2)] for k in range(2 * nx)]
    for d in near_first(nz):
        bcs[d].wait_recv()
    for one in va.values():
        one.wait_recv()
    pick(vx, vsel)
    vb = {}
    for d in near_first(ny):
        vb[d] = go(vsel.at[(y + d) % ny], vy.at[y], "vb", d, to_y(d))
    vy[y] = vsel[y]

    for d in near_first(ny):
        ly[d].wait_recv()
        forward_l(d)

    for d in near_first(ny):
        vb[d].wait_recv()
    piece = summed(vy, ny)
    vpiece[...] = piece
    vband[x, :, pl.ds(mine, rank)] = piece
    vc = {}
    for d, flip in chips:
        vc[d, flip] = go(
            vpiece, vband.at[x, :, pl.ds(mine, rank)], "vc", 2 * d + flip, to_x(d, flip)
        )

    for one in ua.values():
        one.wait_recv()
    pick(ux, usel)
    ub = {}
    for d in near_first(ny):
        ub[d] = go(usel.at[(y + d) % ny], uy.at[y], "ub", d, to_y(d))
    uy[y] = usel[y]

    for one in vc.values():
        one.wait_recv()
    rows = jnp.concatenate([lbuf[k, x].astype(F32) for k in range(ny)], axis=0).astype(BF)
    part = jnp.dot(rows, vband[...].reshape(width, 2 * rank), preferred_element_type=F32)
    zysend[...] = part.reshape(ny, depth, 2 * rank).astype(BF)
    zy = {}
    for e in near_first(nz):
        zy[e] = go(zysend.at[(z + e) % nz], zyrecv.at[z], "zy", e, to_z(e))
    zyrecv[z] = zysend[z]

    for d in near_first(ny):
        ub[d].wait_recv()
    piece = summed(uy, ny)
    upiece[...] = piece
    ut = copy(upiece, uband.at[h, z, x], "ut", 0, to_turned)

    @pl.when(y != z)
    def _():
        ut.start()

    @pl.when(y == z)
    def _():
        uband[h, z, x] = piece

    cv.wait_recv()
    zs = {}
    for d in order_y:
        yy = (y - d) % ny
        for dx in near_first(nx):
            lx[d, dx].wait_recv()
        block = lbuf[yy].astype(F32).reshape(nx * depth, width).astype(BF)
        part = jnp.dot(block, vchip[...], preferred_element_type=F32)
        part = part.reshape(nx, depth, 2 * rank).astype(BF)
        zsend[d] = part
        e = (yy + nz - z) % nz
        zs[d] = copy(zsend.at[d], zrecv.at[z], "zs", d, {"row": row, "col": yy}, rk=e)

        @pl.when(e != 0)
        def _():
            zs[d].start()

        @pl.when(e == 0)
        def _():
            zrecv[z] = part

    @pl.when(y != z)
    def _():
        ut.wait_recv()

    ud = {}
    for d in near_first(ny):
        ud[d] = go(uband.at[h, y, x], uband.at[h, y, x], "ud", d, to_y(d))

    for e in near_first(nz):
        zy[e].wait_recv()
    acc = zyrecv[0].astype(F32)
    for k in range(1, nz):
        acc = acc + zyrecv[k].astype(F32)
    yg[x, y] = acc.astype(BF)
    gy, gx = {}, {}
    for d in near_first(ny):
        gy[d] = go(yg.at[x, y], yg.at[x, y], "gy", d, to_y(d))

    def forward_g(d):
        yy = (y - d) % ny
        for dx in near_first(nx):
            gx[d, dx] = go(yg.at[x, yy], yg.at[x, yy], "gx", d * nx + dx, to_x(dx))

    forward_g(0)
    for d in near_first(ny):
        gy[d].wait_recv()
        forward_g(d)

    for d in near_first(ny):
        ud[d].wait_recv()
    ue = {}
    for d in near_first(nx):
        ue[d] = go(uband.at[h, :, x], uband.at[h, :, x], "ue", d, to_x(d))

    for e in range(1, nz):
        copy(zsend.at[0], zrecv.at[z], "zs", 0, to_z(1), rk=e).wait_recv()
    acc = zrecv[0].astype(F32)
    for k in range(1, nz):
        acc = acc + zrecv[k].astype(F32)
    sol[...] = acc.reshape(nx * depth, 2 * rank).astype(BF)

    pc, zc = {}, {}

    def partial_core(d):
        p = (y - d) % ny
        for dx in near_first(nx):
            gx[d, dx].wait_recv()
        y_rows = jnp.concatenate([yg[k, p].astype(F32) for k in range(nx)], axis=0).astype(BF)
        part = cross_rows(sol[...], y_rows)
        low, high = part[:rank], part[rank:]
        pown[d] = jnp.where(h == 0, low, high)
        psend[d] = jnp.where(h == 0, high, low)
        pc[d] = go(psend.at[d], psib.at[d], "pc", d, to_sib)

    def send_core(d):
        p = (y - d) % ny
        e = (p + nz - z) % nz
        pc[d].wait_recv()
        csum = (pown[d] + psib[d]).astype(BF)
        csend[d] = csum
        zc[d] = copy(csend.at[d], crecv.at[z], "zc", d, {"row": row, "col": p}, rk=e)

        @pl.when(e != 0)
        def _():
            zc[d].start()

        @pl.when(e == 0)
        def _():
            crecv[z] = csum

    lag = 2
    for k, d in enumerate(order_y):
        partial_core(d)
        if k >= lag:
            send_core(order_y[k - lag])
    for d in order_y[-lag:]:
        send_core(d)

    for d in near_first(nx):
        ue[d].wait_recv()
    uf = go(uband.at[h], uband.at[h], "uf", 0, to_sib)

    keeps = [
        flag_row((1, rank), lanes < rank_map[own_tile, band_cols[i]]).astype(BF) for i in range(2)
    ]

    def gram(out_ref, at, kept_ref, i, other):
        out_ref[at] = jnp.zeros((2 * rank, 2 * rank), F32)

        def body(k, carry):
            part = pl.ds(pl.multiple_of(k * width, 16), width)
            both = jnp.concatenate([kept_ref[i, part, :] * keeps[i], other(k, part)], axis=1)
            out_ref[at] += cross_rows(both, both)
            return carry

        lax.fori_loop(0, points // width, body, 0)

    load_tu.wait()
    for i in range(2):
        gram(gram_left, (0, i), tu, i, lambda k, part: basis[part, :])
    load_tv.wait()
    uf.wait_recv()
    for i in range(2):
        gram(right, (i,), tv, i, lambda k, part: uband[i, k].reshape(width, rank))

    for e in range(1, nz):
        copy(csend.at[0], crecv.at[z], "zc", 0, to_z(1), rk=e).wait_recv()
    core = crecv[0].astype(F32)
    for k in range(1, nz):
        core = core + crecv[k].astype(F32)

    def times_transposed(first, second):
        return lax.dot_general(
            first, second, (((1,), (1,)), ((), ())), precision=HI, preferred_element_type=F32
        )

    for i in range(2):
        lower = flag_row((1, rank), jnp.broadcast_to(band_cols[i] < own_tile, (1, rank)))
        c = core[:, i * rank:(i + 1) * rank] * lower
        g = right[i, :rank, rank:]
        half = jnp.dot(c, right[i, rank:, rank:], precision=HI, preferred_element_type=F32)
        gram_right[0, i, :rank, :rank] = right[i, :rank, :rank]
        gram_right[0, i, :rank, rank:] = -times_transposed(g, c)
        gram_right[0, i, rank:, :rank] = -times_transposed(c, g)
        gram_right[0, i, rank:, rank:] = times_transposed(half, c)

    for one in started:
        one.wait_send()

    @pl.when(y != z)
    def _():
        ut.wait_send()

    for d in order_y:

        @pl.when(((y - d) % ny + nz - z) % nz != 0)
        def _():
            zs[d].wait_send()
            zc[d].wait_send()


def shards(dims, panel_u, panel_v, linv, trail_u, trail_v, rank_map, tile_of_slot, band_cols):
    ny, nx, nz = dims
    points, rank = panel_u.shape[1:]
    depth, width = linv.shape
    py = width // nx
    _, total = plan(ny, nx, nz)
    vmem = pl.BlockSpec(memory_space=pltpu.VMEM)
    smem = pl.BlockSpec(memory_space=pltpu.SMEM)
    hbm = pl.BlockSpec(memory_space=pl.ANY)
    out = jax.ShapeDtypeStruct((1, 2, 2 * rank, 2 * rank), F32)
    scratch = [
        pltpu.VMEM((points, rank), BF),
        pltpu.VMEM((width, rank), BF),
        pltpu.VMEM((width, 2 * rank), BF),
        pltpu.VMEM((nx, 2, py, rank), BF),
        pltpu.VMEM((nz, py, rank), BF),
        pltpu.VMEM((ny, py, rank), BF),
        pltpu.VMEM((py, rank), BF),
        pltpu.VMEM((nx, py, 2 * rank), BF),
        pltpu.VMEM((nx, 2, py, rank), BF),
        pltpu.VMEM((nz, py, rank), BF),
        pltpu.VMEM((ny, py, rank), BF),
        pltpu.VMEM((py, rank), BF),
        pltpu.VMEM((2, nz, nx, py, rank), BF),
        pltpu.VMEM((2, points, rank), BF),
        pltpu.VMEM((2, points, rank), BF),
        pltpu.VMEM((ny, nx, depth, width), BF),
        pltpu.VMEM((ny, nx, depth, 2 * rank), BF),
        pltpu.VMEM((nz, nx, depth, 2 * rank), BF),
        pltpu.VMEM((nx * depth, 2 * rank), BF),
        pltpu.VMEM((nz, depth, 2 * rank), BF),
        pltpu.VMEM((nz, depth, 2 * rank), BF),
        pltpu.VMEM((nx, ny, depth, 2 * rank), BF),
        pltpu.VMEM((nz, 8, rank), jnp.int32),
        pltpu.VMEM((ny, rank, 2 * rank), F32),
        pltpu.VMEM((ny, rank, 2 * rank), F32),
        pltpu.VMEM((ny, rank, 2 * rank), F32),
        pltpu.VMEM((ny, rank, 2 * rank), BF),
        pltpu.VMEM((nz, rank, 2 * rank), BF),
        pltpu.VMEM((2, 2 * rank, 2 * rank), F32),
        pltpu.SemaphoreType.DMA((total,)),
        pltpu.SemaphoreType.DMA((total,)),
        pltpu.SemaphoreType.DMA((5,)),
    ]
    return pl.pallas_call(
        functools.partial(kernel, dims),
        out_shape=(out, out),
        in_specs=[hbm, hbm, hbm, hbm, hbm, smem, smem, smem],
        out_specs=(vmem, vmem),
        scratch_shapes=scratch,
        compiler_params=pltpu.CompilerParams(
            collective_id=0, has_side_effects=True, vmem_limit_bytes=60 * 2**20
        ),
    )(panel_u, panel_v, linv, trail_u, trail_v, rank_map, tile_of_slot, band_cols)


def solution(mesh):
    nz = mesh.shape["col"]
    ny = nz
    nx = mesh.shape["row"] // (2 * ny)
    return jax.shard_map(
        functools.partial(shards, (ny, nx, nz)),
        mesh=mesh,
        in_specs=(
            P("row", None, None),
            P("row", "col", None),
            P("row", "col"),
            P("row", "col", None, None),
            P("row", "col", None, None),
            P(),
            P(),
            P("col"),
        ),
        out_specs=(P("row", "col", None, None), P("row", "col", None, None)),
        check_vma=False,
    )
```

time: 377 us -> 82.7 us (0.22)
  the two profiles are of different devices: /device:TPU:25 before, /device:TPU:192 now
where the time goes in v2:
time: 82.7 us; the launch traced here: 82.4 us
  Pallas kernels  79.1 us (96%)
  local copies, waits for them, and re-layouts  2.72 us (3%)
    pallas_call x1, Pallas kernels, shards(): pl.pallas_call(functools.partial(kernel, dims), out_shape=(out, out), in_...  79.1 us
    unnamed x4, local copies, waits for them, and re-layouts  2.72 us

profile of v2, /device:TPU:192, one launch (start us, length us, event | category | flops | bytes accessed | tf_op | source)
XLA Modules:
  0.0 82.4 jit_solution(1493715418962876436)
XLA Ops:
  0.6 79.1 %shard_map.95 = (f32[1,2,256,256]{3,2,1,0:T(8,128)}, f32[1,2,256,256]{3,2,1,0:T(8,128)}) custom-call(bf16[1,2560,128]{2,1,0:T(8,128)(2,1)} %panel_u.1, bf16[1,320,128]{2,1,0:T(8,128)(2,1)} %panel_v.1, bf16[40,320]{1,0:T(8,128)(2,1)} %linv.1, bf16[1,2,2560,128]{3,2,1,0:T(8,128)(2,1)} %trail_u.1, bf16[1,2,2560,128]{3,2,1,0:T(8,128)(2,1)} %trail_v.1, ...), custom_call_target="tpu_custom_call" | custom-call | tf_op jit(solution)/shard_map/pallas_call | solution.py:440
  79.7 0.0 copy-start
  79.7 1.9 %copy.12 = f32[1,2,256,256]{3,2,1,0:T(8,128)} copy(f32[1,2,256,256]{3,2,1,0:T(8,128)} %get-tuple-element.4) | data formatting | bytes 1048576
  81.6 0.0 copy-done
  81.6 0.8 copy.13
Async XLA Ops:
  79.7 1.9 %copy-start = (f32[1,2,256,256]{3,2,1,0:T(8,128)S(1)}, f32[1,2,256,256]{3,2,1,0:T(8,128)}, u32[]{:S(2)}) copy-start(f32[1,2,256,256]{3,2,1,0:T(8,128)} %get-tuple-element.5) | copy-start | bytes 1572868

commit v3 on v2

--- a/solution.py
+++ b/solution.py
@@ -217,20 +217,6 @@
         zy[e] = go(zysend.at[(z + e) % nz], zyrecv.at[z], "zy", e, to_z(e))
     zyrecv[z] = zysend[z]
 
-    for d in near_first(ny):
-        ub[d].wait_recv()
-    piece = summed(uy, ny)
-    upiece[...] = piece
-    ut = copy(upiece, uband.at[h, z, x], "ut", 0, to_turned)
-
-    @pl.when(y != z)
-    def _():
-        ut.start()
-
-    @pl.when(y == z)
-    def _():
-        uband[h, z, x] = piece
-
     cv.wait_recv()
     zs = {}
     for d in order_y:
@@ -252,13 +238,19 @@
         def _():
             zrecv[z] = part
 
+    for d in near_first(ny):
+        ub[d].wait_recv()
+    piece = summed(uy, ny)
+    upiece[...] = piece
+    ut = copy(upiece, uband.at[h, z, x], "ut", 0, to_turned)
+
     @pl.when(y != z)
     def _():
-        ut.wait_recv()
-
-    ud = {}
-    for d in near_first(ny):
-        ud[d] = go(uband.at[h, y, x], uband.at[h, y, x], "ud", d, to_y(d))
+        ut.start()
+
+    @pl.when(y == z)
+    def _():
+        uband[h, z, x] = piece
 
     for e in near_first(nz):
         zy[e].wait_recv()
@@ -276,6 +268,15 @@
             gx[d, dx] = go(yg.at[x, yy], yg.at[x, yy], "gx", d * nx + dx, to_x(dx))
 
     forward_g(0)
+
+    @pl.when(y != z)
+    def _():
+        ut.wait_recv()
+
+    ud = {}
+    for d in near_first(ny):
+        ud[d] = go(uband.at[h, y, x], uband.at[h, y, x], "ud", d, to_y(d))
+
     for d in near_first(ny):
         gy[d].wait_recv()
         forward_g(d)
@@ -334,16 +335,13 @@
         ue[d].wait_recv()
     uf = go(uband.at[h], uband.at[h], "uf", 0, to_sib)
 
-    keeps = [
-        flag_row((1, rank), lanes < rank_map[own_tile, band_cols[i]]).astype(BF) for i in range(2)
-    ]
-
     def gram(out_ref, at, kept_ref, i, other):
         out_ref[at] = jnp.zeros((2 * rank, 2 * rank), F32)
+        keep = flag_row((1, rank), lanes < rank_map[own_tile, band_cols[i]]).astype(BF)
 
         def body(k, carry):
             part = pl.ds(pl.multiple_of(k * width, 16), width)
-            both = jnp.concatenate([kept_ref[i, part, :] * keeps[i], other(k, part)], axis=1)
+            both = jnp.concatenate([kept_ref[i, part, :] * keep, other(k, part)], axis=1)
             out_ref[at] += cross_rows(both, both)
             return carry
 
@@ -353,9 +351,10 @@
     for i in range(2):
         gram(gram_left, (0, i), tu, i, lambda k, part: basis[part, :])
     load_tv.wait()
+    gram(right, (h,), tv, h, lambda k, part: uband[h, k].reshape(width, rank))
     uf.wait_recv()
-    for i in range(2):
-        gram(right, (i,), tv, i, lambda k, part: uband[i, k].reshape(width, rank))
+    other = 1 - h
+    gram(right, (other,), tv, other, lambda k, part: uband[other, k].reshape(width, rank))
 
     for e in range(1, nz):
         copy(csend.at[0], crecv.at[z], "zc", 0, to_z(1), rk=e).wait_recv()

time: 82.7 us -> 82.8 us (level)
  no operation moved by 1% of the time
where the time goes in v3:
time: 82.8 us; the launch traced here: 82.5 us
  Pallas kernels  79.1 us (96%)
  local copies, waits for them, and re-layouts  2.72 us (3%)
    pallas_call x1, Pallas kernels, shards(): pl.pallas_call(functools.partial(kernel, dims), out_shape=(out, out), in_...  79.1 us
    unnamed x4, local copies, waits for them, and re-layouts  2.72 us

profile of v3, /device:TPU:192, one launch (start us, length us, event | category | flops | bytes accessed | tf_op | source)
XLA Modules:
  0.0 82.5 jit_solution(4270472666877700126)
XLA Ops:
  0.6 79.1 %shard_map.95 = (f32[1,2,256,256]{3,2,1,0:T(8,128)}, f32[1,2,256,256]{3,2,1,0:T(8,128)}) custom-call(bf16[1,2560,128]{2,1,0:T(8,128)(2,1)} %panel_u.1, bf16[1,320,128]{2,1,0:T(8,128)(2,1)} %panel_v.1, bf16[40,320]{1,0:T(8,128)(2,1)} %linv.1, bf16[1,2,2560,128]{3,2,1,0:T(8,128)(2,1)} %trail_u.1, bf16[1,2,2560,128]{3,2,1,0:T(8,128)(2,1)} %trail_v.1, ...), custom_call_target="tpu_custom_call" | custom-call | tf_op jit(solution)/shard_map/pallas_call | solution.py:439
  79.8 0.0 copy-start
  79.8 1.9 %copy.12 = f32[1,2,256,256]{3,2,1,0:T(8,128)} copy(f32[1,2,256,256]{3,2,1,0:T(8,128)} %get-tuple-element.4) | data formatting | bytes 1048576
  81.7 0.0 copy-done
  81.7 0.8 copy.13
Async XLA Ops:
  79.8 1.9 %copy-start = (f32[1,2,256,256]{3,2,1,0:T(8,128)S(1)}, f32[1,2,256,256]{3,2,1,0:T(8,128)}, u32[]{:S(2)}) copy-start(f32[1,2,256,256]{3,2,1,0:T(8,128)} %get-tuple-element.5) | copy-start | bytes 1572868

commit v4 on v3

--- a/solution.py
+++ b/solution.py
@@ -185,10 +185,6 @@
     vy[y] = vsel[y]
 
     for d in near_first(ny):
-        ly[d].wait_recv()
-        forward_l(d)
-
-    for d in near_first(ny):
         vb[d].wait_recv()
     piece = summed(vy, ny)
     vpiece[...] = piece
@@ -198,6 +194,10 @@
         vc[d, flip] = go(
             vpiece, vband.at[x, :, pl.ds(mine, rank)], "vc", 2 * d + flip, to_x(d, flip)
         )
+
+    for d in near_first(ny):
+        ly[d].wait_recv()
+        forward_l(d)
 
     for one in ua.values():
         one.wait_recv()

time: 82.8 us -> 81.2 us (0.981)
  the two profiles are of different devices: /device:TPU:192 before, /device:TPU:72 now
where the time goes in v4:
time: 81.2 us; the launch traced here: 80.9 us
  Pallas kernels  77.5 us (95%)
  local copies, waits for them, and re-layouts  2.72 us (3%)
    pallas_call x1, Pallas kernels, shards(): pl.pallas_call(functools.partial(kernel, dims), out_shape=(out, out), in_...  77.5 us
    unnamed x4, local copies, waits for them, and re-layouts  2.72 us

profile of v4, /device:TPU:72, one launch (start us, length us, event | category | flops | bytes accessed | tf_op | source)
XLA Modules:
  0.0 80.9 jit_solution(11522628915860525948)
XLA Ops:
  0.6 77.5 %shard_map.95 = (f32[1,2,256,256]{3,2,1,0:T(8,128)}, f32[1,2,256,256]{3,2,1,0:T(8,128)}) custom-call(bf16[1,2560,128]{2,1,0:T(8,128)(2,1)} %panel_u.1, bf16[1,320,128]{2,1,0:T(8,128)(2,1)} %panel_v.1, bf16[40,320]{1,0:T(8,128)(2,1)} %linv.1, bf16[1,2,2560,128]{3,2,1,0:T(8,128)(2,1)} %trail_u.1, bf16[1,2,2560,128]{3,2,1,0:T(8,128)(2,1)} %trail_v.1, ...), custom_call_target="tpu_custom_call" | custom-call | tf_op jit(solution)/shard_map/pallas_call | solution.py:439
  78.2 0.0 copy-start
  78.2 1.9 %copy.12 = f32[1,2,256,256]{3,2,1,0:T(8,128)} copy(f32[1,2,256,256]{3,2,1,0:T(8,128)} %get-tuple-element.4) | data formatting | bytes 1048576
  80.1 0.0 copy-done
  80.1 0.8 copy.13
Async XLA Ops:
  78.2 1.9 %copy-start = (f32[1,2,256,256]{3,2,1,0:T(8,128)S(1)}, f32[1,2,256,256]{3,2,1,0:T(8,128)}, u32[]{:S(2)}) copy-start(f32[1,2,256,256]{3,2,1,0:T(8,128)} %get-tuple-element.5) | copy-start | bytes 1572868
